TPU v7x, 32 devices: a whole 2x2x4 slice. The times are simulated.
32 devices in a mesh: gx: 2 (over x), gy: 4 (over y, core), gz: 4 (over z).
Axes of the slice: x: 2, y: 2, z: 4, core: 2. Of those that a mesh axis runs over, the one named last changes fastest.
Arguments:
- pre_act: bfloat16 [512, 24576], P('gx', ('gy', 'gz')), may hold values from -6 to 6
- grad_out: bfloat16 [512, 6144], P(('gx', 'gy'), 'gz'), may hold values from -0.625 to 0.625
- weight: bfloat16 [12288, 2, 6144], P('gy', 'gx', 'gz'), may hold values from -4 to 4
Outputs:
- pre_grad: bfloat16 [512, 24576], P('gx', ('gy', 'gz'))
- weight_grad: bfloat16 [12288, 2, 6144], P('gy', 'gx', 'gz')
All inputs are finite; a program needn't handle non-finite values.
Results may differ from a plain program's by a relative error of at most 0.02.
Values may be sent and summed in bfloat16 or wider, within the bound.
A program may use at most 128 MiB of HBM per device.

v0:
```python
import functools

import jax
import jax.numpy as jnp
from jax import lax
from jax.experimental import pallas as pl
from jax.experimental.pallas import tpu as pltpu
from jax.sharding import PartitionSpec as P

tanh_scale = 0.7978845608028654
cubic_coef = 0.044715
MESH = pl.DeviceIdType.MESH
UP, DOWN = 0, 1


def gelu_parts(inputs):
    inner = tanh_scale * (inputs + cubic_coef * inputs * inputs * inputs)
    tangent = jnp.tanh(inner)
    gelu_value = 0.5 * inputs * (1.0 + tangent)
    gelu_slope = 0.5 * (1.0 + tangent) + 0.5 * inputs * (1.0 - tangent * tangent) * tanh_scale * (
        1.0 + 3.0 * cubic_coef * inputs * inputs
    )
    return (gelu_value, gelu_slope)


def pick(me, values):
    out = jnp.int32(values[0])
    for at in range(1, len(values)):
        out = jnp.where(me == at, jnp.int32(values[at]), out)
    return out


def exchange_kernel(
    pre_ref,
    grad_ref,
    weight_ref,
    pre_grad_ref,
    weight_grad_ref,
    weight_vmem,
    pre_vmem,
    rows,
    hidden,
    other_part,
    slope,
    part,
    arrived,
    outgoing,
    final,
    load_sem,
    grad_send,
    grad_recv,
    x_send,
    x_recv,
    ag_send,
    ag_recv,
    rs_send,
    rs_recv,
):
    gx, gy, me = lax.axis_index("gx"), lax.axis_index("gy"), lax.axis_index("gz")
    other_x = 1 - gx
    core = gy + 1 - 2 * lax.rem(gy, 2)
    far_y = lax.rem(gy + 2, 4)
    is_mid = jnp.logical_and(me > 0, me < 3)
    is_end = jnp.logical_not(is_mid)
    tokens, cols = pre_ref.shape
    block = grad_ref.shape[0]
    width = grad_ref.shape[1]
    units = cols // 2

    barrier = pltpu.get_barrier_semaphore()
    for peer in ({"gy": core}, {"gx": other_x}, {"gy": far_y}):
        pl.semaphore_signal(barrier, inc=1, device_id=peer, device_id_type=MESH)

    @pl.when(me > 0)
    def _():
        pl.semaphore_signal(barrier, inc=1, device_id={"gz": me - 1}, device_id_type=MESH)

    @pl.when(me < 3)
    def _():
        pl.semaphore_signal(barrier, inc=1, device_id={"gz": me + 1}, device_id_type=MESH)

    own_rows = rows.at[gx, pl.ds(pl.multiple_of(gy * block, block), block), :]
    pre_load = pltpu.make_async_copy(pre_ref, pre_vmem, load_sem.at[0])
    pre_load.start()
    grad_load = pltpu.make_async_copy(grad_ref, own_rows, load_sem.at[1])
    grad_load.start()
    weight_load = pltpu.make_async_copy(weight_ref, weight_vmem, load_sem.at[2])
    weight_load.start()
    pl.semaphore_wait(barrier, jnp.where(is_mid, 5, 4))

    def grad_copy(kind, bx, by, peer, src=None):
        at = rows.at[bx, pl.ds(pl.multiple_of(by * block, block), block), :]
        return pltpu.make_async_remote_copy(
            src_ref=at if src is None else src,
            dst_ref=at,
            send_sem=grad_send.at[kind],
            recv_sem=grad_recv.at[kind],
            device_id=peer,
            device_id_type=MESH,
        )

    to_x = grad_copy(1, gx, gy, {"gx": other_x}, grad_ref)
    to_y = grad_copy(2, gx, gy, {"gy": far_y}, grad_ref)
    to_core = grad_copy(0, gx, gy, {"gy": core}, grad_ref)
    to_x.start()
    to_y.start()
    to_core.start()
    pre_load.wait()

    group = 256
    half = group // 2
    line = lax.broadcasted_iota(jnp.int32, (group, group), 0)
    lane = lax.broadcasted_iota(jnp.int32, (group, group), 1)
    target = jnp.where(line < half, 2 * line + gx, 2 * (line - half) + other_x)
    select = jnp.where(lane == target, 1.0, 0.0).astype(jnp.bfloat16)
    for q in range(cols // group):
        span = slice(q * group, (q + 1) * group)
        value, slope_part = gelu_parts(pre_vmem[:, span].astype(jnp.float32))
        slope[:, span] = slope_part
        moved = lax.dot_general(
            select,
            value.astype(jnp.bfloat16),
            (((1,), (1,)), ((), ())),
            preferred_element_type=jnp.float32,
        ).astype(jnp.bfloat16)
        hidden[gx, me, q * half : (q + 1) * half, :] = moved[:half]
        other_part[q * half : (q + 1) * half, :] = moved[half:]

    def remote(src, dst, send, recv, peer):
        return pltpu.make_async_remote_copy(
            src_ref=src,
            dst_ref=dst,
            send_sem=send,
            recv_sem=recv,
            device_id=peer,
            device_id_type=MESH,
        )

    def ag(way, second, hop):
        step = 1 - 2 * way
        owner = me - hop * step
        tok = other_x if second else gx
        at = hidden.at[tok, owner]
        return remote(at, at, ag_send.at[way, second, hop], ag_recv.at[way, second, hop], {"gz": me + step})

    def ag_arrival(way, second, hop):
        step = 1 - 2 * way
        owner = me - step - hop * step
        tok = other_x if second else gx
        at = hidden.at[tok, owner]
        return remote(at, at, ag_send.at[way, second, hop], ag_recv.at[way, second, hop], {"gz": me - step})

    def both_ways(second):
        @pl.when(me < 3)
        def _():
            ag(UP, second, 0).start()

        @pl.when(me > 0)
        def _():
            ag(DOWN, second, 0).start()

    x_hidden = remote(other_part, hidden.at[gx, me], x_send.at[0], x_recv.at[0], {"gx": other_x})
    x_hidden_in = remote(other_part, hidden.at[other_x, me], x_send.at[0], x_recv.at[0], {"gx": other_x})
    x_hidden.start()
    both_ways(0)

    to_x.wait_recv()
    x_to_y = grad_copy(3, other_x, gy, {"gy": far_y})
    x_to_y.start()
    x_to_core = grad_copy(4, other_x, gy, {"gy": core})
    x_to_core.start()
    to_y.wait_recv()
    y_to_core = grad_copy(5, gx, far_y, {"gy": core})
    y_to_core.start()
    x_to_y.wait_recv()
    diag_to_core = grad_copy(6, other_x, far_y, {"gy": core})
    diag_to_core.start()
    for copy in (to_core, x_to_core, y_to_core, diag_to_core):
        copy.wait_recv()
    grad_load.wait()

    far = pick(me, (UP, UP, DOWN, DOWN))
    near = 1 - far

    def pass_on(way, second, hop):
        ag_arrival(way, second, hop - 1).wait_recv()
        ag(way, second, hop).start()

    @pl.when(is_mid)
    def _():
        pass_on(far, 0, 1)
        pass_on(near, 0, 1)

    goal = (
        pick(me, (3, 3, 0, 0)),
        pick(me, (2, 2, 1, 1)),
        pick(me, (1, 0, 3, 2)),
        me,
    )
    way = (far, far, pick(me, (UP, DOWN, UP, DOWN)))
    tile = 256
    tiles = units // tile
    weight_load.wait()

    def compute(index, carry):
        slot = index // tiles
        piece = lax.rem(index, tiles)
        step = slot // 2
        tok = jnp.where(lax.rem(slot, 2) == 0, other_x, gx)
        to = jnp.where(step == 0, goal[0], jnp.where(step == 1, goal[1], jnp.where(step == 2, goal[2], me)))
        here = weight_vmem[pl.ds(pl.multiple_of(to * units + piece * tile, tile), tile), :]
        part[slot, :, pl.ds(pl.multiple_of(piece * tile, tile), tile)] = lax.dot_general(
            rows[tok], here, (((1,), (1,)), ((), ())), preferred_element_type=jnp.float32
        )
        return carry

    def rs(step, second):
        to, where = goal[step], way[step]
        return remote(
            outgoing.at[2 * step + second],
            arrived.at[where, to, second],
            rs_send.at[2 * step + second],
            rs_recv.at[where, to, second],
            {"gz": me + 1 - 2 * where},
        )

    def rs_arrival(where, to, second):
        at = arrived.at[where, to, second]
        return remote(
            at,
            at,
            rs_send.at[2 * 0 + second],
            rs_recv.at[where, to, second],
            {"gz": me - 1 + 2 * where},
        )

    def rs_first(step, second):
        outgoing[2 * step + second] = part[2 * step + second].astype(jnp.bfloat16)
        rs(step, second).start()

    def rs_add(step, second):
        to, where = goal[step], way[step]
        rs_arrival(where, to, second).wait_recv()
        outgoing[2 * step + second] = (
            part[2 * step + second] + arrived[where, to, second].astype(jnp.float32)
        ).astype(jnp.bfloat16)
        rs(step, second).start()

    lax.fori_loop(0, 2 * tiles, compute, 0)

    @pl.when(is_end)
    def _():
        rs_first(0, 0)

    x_hidden_in.wait_recv()
    both_ways(1)
    lax.fori_loop(2 * tiles, 8 * tiles, compute, 0)

    def weight_grad(owner):
        def one(piece, carry):
            at = pl.ds(pl.multiple_of(piece * tile, tile), tile)
            total = jnp.dot(hidden[0, owner, at, :], rows[0], preferred_element_type=jnp.float32)
            total = total + jnp.dot(hidden[1, owner, at, :], rows[1], preferred_element_type=jnp.float32)
            out = pl.ds(pl.multiple_of(owner * units + piece * tile, tile), tile)
            weight_grad_ref[out, :] = total.astype(jnp.bfloat16)
            return carry

        lax.fori_loop(0, tiles, one, 0)

    def arrived_at_end(hop):
        ag_arrival(near, 0, hop).wait_recv()
        ag_arrival(near, 1, hop).wait_recv()

    @pl.when(is_end)
    def _():
        ag(far, 0, 0).wait_send()
        rs_first(0, 1)
        weight_grad(me)
        rs(0, 0).wait_send()
        rs_first(1, 0)
        ag(far, 1, 0).wait_send()
        rs_first(1, 1)
        arrived_at_end(0)
        weight_grad(pick(me, (1, 1, 2, 2)))
        rs(0, 1).wait_send()
        rs_first(2, 0)
        rs(1, 0).wait_send()
        rs_first(2, 1)
        arrived_at_end(1)
        weight_grad(pick(me, (2, 2, 1, 1)))

    @pl.when(is_mid)
    def _():
        rs_add(0, 0)
        weight_grad(me)
        pass_on(near, 0, 2)
        pass_on(near, 1, 1)
        pass_on(far, 1, 1)
        weight_grad(pick(me, (0, 0, 3, 3)))
        rs_add(0, 1)
        weight_grad(3 - me)
        rs_add(2, 0)
        rs_add(1, 0)
        pass_on(near, 1, 2)
        rs_add(1, 1)
        rs_add(2, 1)

    def settle(second):
        @pl.when(me > 0)
        def _():
            rs_arrival(UP, me, second).wait_recv()
            part[6 + second] = part[6 + second] + arrived[UP, me, second].astype(jnp.float32)

        @pl.when(me < 3)
        def _():
            rs_arrival(DOWN, me, second).wait_recv()
            part[6 + second] = part[6 + second] + arrived[DOWN, me, second].astype(jnp.float32)

    settle(0)
    outgoing[6] = part[6].astype(jnp.bfloat16)
    x_sum = remote(outgoing.at[6], final.at[1], x_send.at[1], x_recv.at[1], {"gx": other_x})
    x_sum_in = remote(outgoing.at[6], final.at[1], x_send.at[1], x_recv.at[1], {"gx": other_x})
    x_sum.start()

    @pl.when(is_end)
    def _():
        arrived_at_end(2)

    weight_grad(goal[0])
    settle(1)
    final[0] = part[7].astype(jnp.bfloat16)
    x_sum_in.wait_recv()
    for q in range(cols // group):
        span = slice(q * group, (q + 1) * group)
        pair = jnp.concatenate(
            [final[0, :, q * half : (q + 1) * half], final[1, :, q * half : (q + 1) * half]], axis=1
        )
        total = jnp.dot(pair, select, preferred_element_type=jnp.float32)
        pre_grad_ref[:, span] = (total * slope[:, span]).astype(jnp.bfloat16)

    @pl.when(is_end)
    def _():
        rs(1, 1).wait_send()
        rs(2, 0).wait_send()
        rs(2, 1).wait_send()

    @pl.when(is_mid)
    def _():
        for second in (0, 1):
            for hop in range(2):
                ag(far, second, hop).wait_send()
            for hop in range(3):
                ag(near, second, hop).wait_send()
            for step in range(3):
                rs(step, second).wait_send()

    for copy in (to_core, to_x, to_y, x_to_y, x_to_core, y_to_core, diag_to_core, x_hidden, x_sum):
        copy.wait_send()


def exchange(pre_act, grad_out, weight):
    tokens, cols = pre_act.shape
    block, width = grad_out.shape
    units = cols // 2
    bf16, f32 = jnp.bfloat16, jnp.float32
    vmem = pl.BlockSpec(memory_space=pltpu.VMEM)
    in_hbm = pl.BlockSpec(memory_space=pltpu.HBM)
    dma = pltpu.SemaphoreType.DMA
    return pl.pallas_call(
        exchange_kernel,
        out_shape=(
            pltpu.VMEM((tokens, cols), bf16),
            pltpu.VMEM(weight.shape, bf16),
        ),
        in_specs=[in_hbm, in_hbm, in_hbm],
        out_specs=(vmem, vmem),
        scratch_shapes=[
            pltpu.VMEM(weight.shape, bf16),
            pltpu.VMEM((tokens, cols), bf16),
            pltpu.VMEM((2, tokens, width), bf16),
            pltpu.VMEM((2, 4, units, tokens), bf16),
            pltpu.VMEM((units, tokens), bf16),
            pltpu.VMEM((tokens, cols), f32),
            pltpu.VMEM((8, tokens, units), f32),
            pltpu.VMEM((2, 4, 2, tokens, units), bf16),
            pltpu.VMEM((7, tokens, units), bf16),
            pltpu.VMEM((2, tokens, units), bf16),
            dma((3,)),
            dma((7,)),
            dma((7,)),
            dma((2,)),
            dma((2,)),
            dma((2, 2, 3)),
            dma((2, 2, 3)),
            dma((6,)),
            dma((2, 4, 2)),
        ],
        compiler_params=pltpu.CompilerParams(
            collective_id=0, has_side_effects=True, vmem_limit_bytes=53 * 1024 * 1024
        ),
        name="exchange",
    )(pre_act, grad_out, weight)


def with_kernel(pre_act, grad_out, weight):
    pre_grad, weight_grad = exchange(pre_act, grad_out, weight[:, 0, :])
    return (pre_grad, weight_grad[:, None, :])


def with_collectives(pre_act, grad_out, weight):
    groups = lax.axis_size("gx")
    tokens, cols = pre_act.shape
    value, slope = gelu_parts(pre_act.astype(jnp.float32))
    split = value.astype(jnp.bfloat16).reshape(tokens, cols // groups, groups).transpose(2, 0, 1)
    hidden = lax.all_to_all(split, "gx", 0, 0, tiled=True)
    hidden = lax.all_gather(hidden, "gz", axis=2, tiled=True)
    hidden = hidden.reshape(groups * tokens, -1)
    grad_rows = lax.all_gather(grad_out, ("gx", "gy"), axis=0, tiled=True)
    partial = jnp.einsum("pd,rd->pr", grad_rows, weight[:, 0, :], preferred_element_type=jnp.float32)
    summed = lax.psum_scatter(partial.astype(jnp.bfloat16), "gz", scatter_dimension=1, tiled=True)
    summed = lax.all_to_all(summed.reshape(groups, tokens, -1), "gx", 0, 0, tiled=True)
    summed = summed.transpose(1, 2, 0).reshape(tokens, cols).astype(jnp.float32)
    pre_grad = (summed * slope).astype(jnp.bfloat16)
    weight_grad = jnp.einsum("pr,pd->rd", hidden, grad_rows, preferred_element_type=jnp.float32)
    return (pre_grad, weight_grad.astype(jnp.bfloat16)[:, None, :])


def solution(mesh):
    sizes = tuple(mesh.shape[name] for name in ("gx", "gy", "gz"))
    placed = (P("gx", ("gy", "gz")), P(("gx", "gy"), "gz"), P("gy", "gx", "gz"))
    return jax.shard_map(
        with_kernel if sizes == (2, 4, 4) else with_collectives,
        mesh=mesh,
        in_specs=placed,
        out_specs=(P("gx", ("gy", "gz")), P("gy", "gx", "gz")),
        check_vma=False,
    )
```

profile of v0, /device:TPU:17, one launch (start us, length us, event | category | flops | bytes accessed | tf_op | source)
XLA Modules:
  0.0 86.5 jit_solution(798671278968540445)
XLA Ops:
  0.6 81.3 %exchange.1 = (bf16[256,1536]{1,0:T(8,128)(2,1)S(1)}, bf16[3072,1536]{1,0:T(8,128)(2,1)S(1)}) custom-call(bf16[256,1536]{1,0:T(8,128)(2,1)} %pre_ref.1, bf16[64,1536]{1,0:T(8,128)(2,1)} %grad_ref.1, bf16[3072,1536]{1,0:T(8,128)(2,1)} %bitcast.3), custom_call_target="tpu_custom_call" | custom-call | tf_op jit(solution)/shard_map/exchange/pallas_call | solution.py:369
  81.9 0.9 %copy.7 = bf16[256,1536]{1,0:T(8,128)(2,1)} copy(bf16[256,1536]{1,0:T(8,128)(2,1)S(1)} %get-tuple-element.6) | data formatting | bytes 1572864
  82.8 3.7 %copy.8 = bf16[3072,1,1536]{2,0,1:T(8,128)(2,1)} copy(bf16[3072,1,1536]{2,0,1:T(8,128)(2,1)S(1)} %bitcast.2) | data formatting | bytes 18874368
where the time goes:
time: 86.7 us; the launch traced here: 86.5 us
  Pallas kernels  81.3 us (94%)
  local copies, waits for them, and re-layouts  4.62 us (5%)
    pallas_call x1, Pallas kernels, exchange(): pl.pallas_call(exchange_kernel, out_shape=(pltpu.VMEM((tokens, cols), bf1...  81.3 us
    unnamed x2, local copies, waits for them, and re-layouts  4.62 us

commit v1 on v0

--- a/solution.py
+++ b/solution.py
@@ -34,18 +34,17 @@
     pre_ref,
     grad_ref,
     weight_ref,
-    pre_grad_ref,
     weight_grad_ref,
+    final,
+    slope,
     weight_vmem,
     pre_vmem,
     rows,
     hidden,
     other_part,
-    slope,
     part,
     arrived,
     outgoing,
-    final,
     load_sem,
     grad_send,
     grad_recv,
@@ -86,7 +85,6 @@
     grad_load.start()
     weight_load = pltpu.make_async_copy(weight_ref, weight_vmem, load_sem.at[2])
     weight_load.start()
-    pl.semaphore_wait(barrier, jnp.where(is_mid, 5, 4))
 
     def grad_copy(kind, bx, by, peer, src=None):
         at = rows.at[bx, pl.ds(pl.multiple_of(by * block, block), block), :]
@@ -99,24 +97,15 @@
             device_id_type=MESH,
         )
 
-    to_x = grad_copy(1, gx, gy, {"gx": other_x}, grad_ref)
-    to_y = grad_copy(2, gx, gy, {"gy": far_y}, grad_ref)
-    to_core = grad_copy(0, gx, gy, {"gy": core}, grad_ref)
-    to_x.start()
-    to_y.start()
-    to_core.start()
-    pre_load.wait()
-
     group = 256
     half = group // 2
     line = lax.broadcasted_iota(jnp.int32, (group, group), 0)
     lane = lax.broadcasted_iota(jnp.int32, (group, group), 1)
     target = jnp.where(line < half, 2 * line + gx, 2 * (line - half) + other_x)
     select = jnp.where(lane == target, 1.0, 0.0).astype(jnp.bfloat16)
-    for q in range(cols // group):
-        span = slice(q * group, (q + 1) * group)
-        value, slope_part = gelu_parts(pre_vmem[:, span].astype(jnp.float32))
-        slope[:, span] = slope_part
+
+    def make_hidden(q):
+        value = gelu_parts(pre_vmem[:, q * group : (q + 1) * group].astype(jnp.float32))[0]
         moved = lax.dot_general(
             select,
             value.astype(jnp.bfloat16),
@@ -126,6 +115,18 @@
         hidden[gx, me, q * half : (q + 1) * half, :] = moved[:half]
         other_part[q * half : (q + 1) * half, :] = moved[half:]
 
+    groups = cols // group
+    pre_load.wait()
+    for q in range(groups // 2):
+        make_hidden(q)
+    pl.semaphore_wait(barrier, jnp.where(is_mid, 5, 4))
+    to_x = grad_copy(1, gx, gy, {"gx": other_x}, grad_ref)
+    to_y = grad_copy(2, gx, gy, {"gy": far_y}, grad_ref)
+    to_core = grad_copy(0, gx, gy, {"gy": core}, grad_ref)
+    to_x.start()
+    to_y.start()
+    to_core.start()
+
     def remote(src, dst, send, recv, peer):
         return pltpu.make_async_remote_copy(
             src_ref=src,
@@ -136,33 +137,47 @@
             device_id_type=MESH,
         )
 
-    def ag(way, second, hop):
+    cut = units // 2
+
+    def hidden_piece(owner, piece):
+        tok = gx if piece < 2 else other_x
+        return hidden.at[tok, owner, pl.ds((piece % 2) * cut, cut), :]
+
+    def ag(way, piece, hop):
         step = 1 - 2 * way
-        owner = me - hop * step
-        tok = other_x if second else gx
-        at = hidden.at[tok, owner]
-        return remote(at, at, ag_send.at[way, second, hop], ag_recv.at[way, second, hop], {"gz": me + step})
-
-    def ag_arrival(way, second, hop):
+        at = hidden_piece(me - hop * step, piece)
+        return remote(at, at, ag_send.at[way, piece, hop], ag_recv.at[way, piece, hop], {"gz": me + step})
+
+    def ag_arrival(way, piece, hop):
         step = 1 - 2 * way
-        owner = me - step - hop * step
-        tok = other_x if second else gx
-        at = hidden.at[tok, owner]
-        return remote(at, at, ag_send.at[way, second, hop], ag_recv.at[way, second, hop], {"gz": me - step})
-
-    def both_ways(second):
+        at = hidden_piece(me - step - hop * step, piece)
+        return remote(at, at, ag_send.at[way, piece, hop], ag_recv.at[way, piece, hop], {"gz": me - step})
+
+    def both_ways(piece):
         @pl.when(me < 3)
         def _():
-            ag(UP, second, 0).start()
+            ag(UP, piece, 0).start()
 
         @pl.when(me > 0)
         def _():
-            ag(DOWN, second, 0).start()
-
-    x_hidden = remote(other_part, hidden.at[gx, me], x_send.at[0], x_recv.at[0], {"gx": other_x})
-    x_hidden_in = remote(other_part, hidden.at[other_x, me], x_send.at[0], x_recv.at[0], {"gx": other_x})
-    x_hidden.start()
+            ag(DOWN, piece, 0).start()
+
+    def x_hidden(piece, tok):
+        span = pl.ds(piece * cut, cut)
+        return remote(
+            other_part.at[span, :],
+            hidden.at[tok, me, span, :],
+            x_send.at[piece],
+            x_recv.at[piece],
+            {"gx": other_x},
+        )
+
     both_ways(0)
+    x_hidden(0, gx).start()
+    for q in range(groups // 2, groups):
+        make_hidden(q)
+    both_ways(1)
+    x_hidden(1, gx).start()
 
     to_x.wait_recv()
     x_to_y = grad_copy(3, other_x, gy, {"gy": far_y})
@@ -182,14 +197,15 @@
     far = pick(me, (UP, UP, DOWN, DOWN))
     near = 1 - far
 
-    def pass_on(way, second, hop):
-        ag_arrival(way, second, hop - 1).wait_recv()
-        ag(way, second, hop).start()
+    def pass_on(way, piece, hop):
+        ag_arrival(way, piece, hop - 1).wait_recv()
+        ag(way, piece, hop).start()
 
     @pl.when(is_mid)
     def _():
-        pass_on(far, 0, 1)
-        pass_on(near, 0, 1)
+        for piece in (0, 1):
+            pass_on(far, piece, 1)
+            pass_on(near, piece, 1)
 
     goal = (
         pick(me, (3, 3, 0, 0)),
@@ -214,47 +230,60 @@
         )
         return carry
 
-    def rs(step, second):
+    rows_cut = tokens // 2
+
+    def part_piece(step, piece):
+        return part.at[2 * step + piece // 2, pl.ds((piece % 2) * rows_cut, rows_cut), :]
+
+    def rs(step, piece):
         to, where = goal[step], way[step]
         return remote(
-            outgoing.at[2 * step + second],
-            arrived.at[where, to, second],
-            rs_send.at[2 * step + second],
-            rs_recv.at[where, to, second],
+            outgoing.at[4 * step + piece],
+            arrived.at[where, to, piece],
+            rs_send.at[4 * step + piece],
+            rs_recv.at[where, to, piece],
             {"gz": me + 1 - 2 * where},
         )
 
-    def rs_arrival(where, to, second):
-        at = arrived.at[where, to, second]
-        return remote(
-            at,
-            at,
-            rs_send.at[2 * 0 + second],
-            rs_recv.at[where, to, second],
-            {"gz": me - 1 + 2 * where},
-        )
+    def rs_arrival(where, to, piece):
+        at = arrived.at[where, to, piece]
+        return remote(at, at, rs_send.at[piece], rs_recv.at[where, to, piece], {"gz": me - 1 + 2 * where})
 
     def rs_first(step, second):
-        outgoing[2 * step + second] = part[2 * step + second].astype(jnp.bfloat16)
-        rs(step, second).start()
+        for piece in (2 * second, 2 * second + 1):
+            outgoing[4 * step + piece] = part_piece(step, piece)[...].astype(jnp.bfloat16)
+            rs(step, piece).start()
+
+    def rs_sent(step, second):
+        for piece in (2 * second, 2 * second + 1):
+            rs(step, piece).wait_send()
 
     def rs_add(step, second):
         to, where = goal[step], way[step]
-        rs_arrival(where, to, second).wait_recv()
-        outgoing[2 * step + second] = (
-            part[2 * step + second] + arrived[where, to, second].astype(jnp.float32)
-        ).astype(jnp.bfloat16)
-        rs(step, second).start()
-
-    lax.fori_loop(0, 2 * tiles, compute, 0)
+        for piece in (2 * second, 2 * second + 1):
+            rs_arrival(where, to, piece).wait_recv()
+            outgoing[4 * step + piece] = (
+                part_piece(step, piece)[...] + arrived[where, to, piece].astype(jnp.float32)
+            ).astype(jnp.bfloat16)
+            rs(step, piece).start()
+
+    lax.fori_loop(0, tiles, compute, 0)
 
     @pl.when(is_end)
     def _():
         rs_first(0, 0)
 
-    x_hidden_in.wait_recv()
-    both_ways(1)
-    lax.fori_loop(2 * tiles, 8 * tiles, compute, 0)
+    for piece in (0, 1):
+        x_hidden(piece, other_x).wait_recv()
+        both_ways(2 + piece)
+    lax.fori_loop(tiles, 8 * tiles, compute, 0)
+
+    def make_slope(q, carry):
+        span = pl.ds(pl.multiple_of(q * group, group), group)
+        slope[:, span] = gelu_parts(pre_vmem[:, span].astype(jnp.float32))[1]
+        return carry
+
+    lax.fori_loop(0, groups, make_slope, 0)
 
     def weight_grad(owner):
         def one(piece, carry):
@@ -268,23 +297,25 @@
         lax.fori_loop(0, tiles, one, 0)
 
     def arrived_at_end(hop):
-        ag_arrival(near, 0, hop).wait_recv()
-        ag_arrival(near, 1, hop).wait_recv()
+        for piece in range(4):
+            ag_arrival(near, piece, hop).wait_recv()
 
     @pl.when(is_end)
     def _():
-        ag(far, 0, 0).wait_send()
+        for piece in (0, 1):
+            ag(far, piece, 0).wait_send()
         rs_first(0, 1)
         weight_grad(me)
-        rs(0, 0).wait_send()
+        rs_sent(0, 0)
         rs_first(1, 0)
-        ag(far, 1, 0).wait_send()
+        for piece in (2, 3):
+            ag(far, piece, 0).wait_send()
         rs_first(1, 1)
         arrived_at_end(0)
         weight_grad(pick(me, (1, 1, 2, 2)))
-        rs(0, 1).wait_send()
+        rs_sent(0, 1)
         rs_first(2, 0)
-        rs(1, 0).wait_send()
+        rs_sent(1, 0)
         rs_first(2, 1)
         arrived_at_end(1)
         weight_grad(pick(me, (2, 2, 1, 1)))
@@ -293,69 +324,80 @@
     def _():
         rs_add(0, 0)
         weight_grad(me)
-        pass_on(near, 0, 2)
-        pass_on(near, 1, 1)
-        pass_on(far, 1, 1)
+        for piece in (0, 1):
+            pass_on(near, piece, 2)
+        for piece in (2, 3):
+            pass_on(near, piece, 1)
+            pass_on(far, piece, 1)
         weight_grad(pick(me, (0, 0, 3, 3)))
         rs_add(0, 1)
         weight_grad(3 - me)
         rs_add(2, 0)
         rs_add(1, 0)
-        pass_on(near, 1, 2)
+        for piece in (2, 3):
+            pass_on(near, piece, 2)
         rs_add(1, 1)
         rs_add(2, 1)
 
-    def settle(second):
+    def settle(piece):
+        total = part_piece(3, piece)
+
         @pl.when(me > 0)
         def _():
-            rs_arrival(UP, me, second).wait_recv()
-            part[6 + second] = part[6 + second] + arrived[UP, me, second].astype(jnp.float32)
+            rs_arrival(UP, me, piece).wait_recv()
+            total[...] = total[...] + arrived[UP, me, piece].astype(jnp.float32)
 
         @pl.when(me < 3)
         def _():
-            rs_arrival(DOWN, me, second).wait_recv()
-            part[6 + second] = part[6 + second] + arrived[DOWN, me, second].astype(jnp.float32)
-
-    settle(0)
-    outgoing[6] = part[6].astype(jnp.bfloat16)
-    x_sum = remote(outgoing.at[6], final.at[1], x_send.at[1], x_recv.at[1], {"gx": other_x})
-    x_sum_in = remote(outgoing.at[6], final.at[1], x_send.at[1], x_recv.at[1], {"gx": other_x})
-    x_sum.start()
+            rs_arrival(DOWN, me, piece).wait_recv()
+            total[...] = total[...] + arrived[DOWN, me, piece].astype(jnp.float32)
+
+        return total[...].astype(jnp.bfloat16)
+
+    def x_sum(piece):
+        return remote(
+            outgoing.at[12 + piece],
+            final.at[1, pl.ds(piece * rows_cut, rows_cut), :],
+            x_send.at[2 + piece],
+            x_recv.at[2 + piece],
+            {"gx": other_x},
+        )
+
+    for piece in (0, 1):
+        outgoing[12 + piece] = settle(piece)
+        x_sum(piece).start()
 
     @pl.when(is_end)
     def _():
         arrived_at_end(2)
 
     weight_grad(goal[0])
-    settle(1)
-    final[0] = part[7].astype(jnp.bfloat16)
-    x_sum_in.wait_recv()
-    for q in range(cols // group):
-        span = slice(q * group, (q + 1) * group)
-        pair = jnp.concatenate(
-            [final[0, :, q * half : (q + 1) * half], final[1, :, q * half : (q + 1) * half]], axis=1
-        )
-        total = jnp.dot(pair, select, preferred_element_type=jnp.float32)
-        pre_grad_ref[:, span] = (total * slope[:, span]).astype(jnp.bfloat16)
+    for piece in (0, 1):
+        final[0, pl.ds(piece * rows_cut, rows_cut), :] = settle(2 + piece)
 
     @pl.when(is_end)
     def _():
-        rs(1, 1).wait_send()
-        rs(2, 0).wait_send()
-        rs(2, 1).wait_send()
+        rs_sent(1, 1)
+        rs_sent(2, 0)
+        rs_sent(2, 1)
 
     @pl.when(is_mid)
     def _():
-        for second in (0, 1):
+        for piece in range(4):
             for hop in range(2):
-                ag(far, second, hop).wait_send()
+                ag(far, piece, hop).wait_send()
             for hop in range(3):
-                ag(near, second, hop).wait_send()
-            for step in range(3):
-                rs(step, second).wait_send()
-
-    for copy in (to_core, to_x, to_y, x_to_y, x_to_core, y_to_core, diag_to_core, x_hidden, x_sum):
+                ag(near, piece, hop).wait_send()
+        for step in range(3):
+            rs_sent(step, 0)
+            rs_sent(step, 1)
+
+    for copy in (to_core, to_x, to_y, x_to_y, x_to_core, y_to_core, diag_to_core):
         copy.wait_send()
+    for piece in (0, 1):
+        x_hidden(piece, gx).wait_send()
+        x_sum(piece).wait_send()
+        x_sum(piece).wait_recv()
 
 
 def exchange(pre_act, grad_out, weight):
@@ -369,41 +411,83 @@
     return pl.pallas_call(
         exchange_kernel,
         out_shape=(
-            pltpu.VMEM((tokens, cols), bf16),
             pltpu.VMEM(weight.shape, bf16),
+            pltpu.VMEM((2, tokens, units), bf16),
+            pltpu.VMEM((tokens, cols), f32),
         ),
         in_specs=[in_hbm, in_hbm, in_hbm],
-        out_specs=(vmem, vmem),
+        out_specs=(vmem, vmem, vmem),
         scratch_shapes=[
             pltpu.VMEM(weight.shape, bf16),
             pltpu.VMEM((tokens, cols), bf16),
             pltpu.VMEM((2, tokens, width), bf16),
             pltpu.VMEM((2, 4, units, tokens), bf16),
             pltpu.VMEM((units, tokens), bf16),
-            pltpu.VMEM((tokens, cols), f32),
             pltpu.VMEM((8, tokens, units), f32),
-            pltpu.VMEM((2, 4, 2, tokens, units), bf16),
-            pltpu.VMEM((7, tokens, units), bf16),
-            pltpu.VMEM((2, tokens, units), bf16),
+            pltpu.VMEM((2, 4, 4, tokens // 2, units), bf16),
+            pltpu.VMEM((14, tokens // 2, units), bf16),
             dma((3,)),
             dma((7,)),
             dma((7,)),
-            dma((2,)),
-            dma((2,)),
-            dma((2, 2, 3)),
-            dma((2, 2, 3)),
-            dma((6,)),
-            dma((2, 4, 2)),
+            dma((4,)),
+            dma((4,)),
+            dma((2, 4, 3)),
+            dma((2, 4, 3)),
+            dma((12,)),
+            dma((2, 4, 4)),
         ],
         compiler_params=pltpu.CompilerParams(
-            collective_id=0, has_side_effects=True, vmem_limit_bytes=53 * 1024 * 1024
+            collective_id=0, has_side_effects=True, vmem_limit_bytes=52 * 1024 * 1024
         ),
         name="exchange",
     )(pre_act, grad_out, weight)
 
 
+def finish_kernel(weight_grad_ref, sums_ref, slope_ref, pre_grad_out, weight_grad_out, pre_grad, sem):
+    own = lax.axis_index("gx")
+    copies = []
+    count = weight_grad_ref.shape[0] // 4
+    for q in range(4):
+        span = pl.ds(q * count, count)
+        copies.append(
+            pltpu.make_async_copy(weight_grad_ref.at[span, :], weight_grad_out.at[span, :], sem.at[q])
+        )
+        copies[-1].start()
+    group = 256
+    half = group // 2
+    line = lax.broadcasted_iota(jnp.int32, (group, group), 0)
+    lane = lax.broadcasted_iota(jnp.int32, (group, group), 1)
+    target = jnp.where(line < half, 2 * line + own, 2 * (line - half) + 1 - own)
+    select = jnp.where(lane == target, 1.0, 0.0).astype(jnp.bfloat16)
+    for q in range(slope_ref.shape[1] // group):
+        span = slice(q * group, (q + 1) * group)
+        pair = jnp.concatenate(
+            [sums_ref[0, :, q * half : (q + 1) * half], sums_ref[1, :, q * half : (q + 1) * half]], axis=1
+        )
+        total = jnp.dot(pair, select, preferred_element_type=jnp.float32)
+        pre_grad[:, span] = (total * slope_ref[:, span]).astype(jnp.bfloat16)
+    copies.append(pltpu.make_async_copy(pre_grad, pre_grad_out, sem.at[4]))
+    copies[-1].start()
+    for copy in copies:
+        copy.wait()
+
+
 def with_kernel(pre_act, grad_out, weight):
-    pre_grad, weight_grad = exchange(pre_act, grad_out, weight[:, 0, :])
+    weight_grad, sums, slope = exchange(pre_act, grad_out, weight[:, 0, :])
+    vmem = pl.BlockSpec(memory_space=pltpu.VMEM)
+    anywhere = pl.BlockSpec(memory_space=pl.ANY)
+    pre_grad, weight_grad = pl.pallas_call(
+        finish_kernel,
+        out_shape=(
+            pltpu.HBM(pre_act.shape, jnp.bfloat16),
+            pltpu.HBM(weight_grad.shape, jnp.bfloat16),
+        ),
+        in_specs=[anywhere, vmem, vmem],
+        out_specs=(anywhere, anywhere),
+        scratch_shapes=[pltpu.VMEM(pre_act.shape, jnp.bfloat16), pltpu.SemaphoreType.DMA((5,))],
+        compiler_params=pltpu.CompilerParams(vmem_limit_bytes=8 * 1024 * 1024),
+        name="finish",
+    )(weight_grad, sums, slope)
     return (pre_grad, weight_grad[:, None, :])
 
 

time: 86.7 us -> 83.5 us (0.963)
  local copies, waits for them, and re-layouts: 4.62 us -> 0 us
  Pallas kernels: 81.3 us -> 82.7 us
    unnamed x2 -> x0, local copies, waits for them, and re-layouts: 4.62 us -> none
    pallas_call x1 -> x2, Pallas kernels: 81.3 us -> 82.7 us  [the longest x1 78.8 us: exchange(): pl.pallas_call(exchange_kernel, out_shape=(pltpu.VMEM(weight.shape, bf16)...]
where the time goes in v1:
time: 83.5 us; the launch traced here: 83.3 us
  Pallas kernels  82.7 us (99%)
    pallas_call x1, Pallas kernels, exchange(): pl.pallas_call(exchange_kernel, out_shape=(pltpu.VMEM(weight.shape, bf16)...  78.8 us
    pallas_call x1, Pallas kernels, with_kernel(): pl.pallas_call(finish_kernel, out_shape=(pltpu.HBM(pre_act.shape, jnp.bfl...  3.9 us

profile of v1, /device:TPU:17, one launch (start us, length us, event | category | flops | bytes accessed | tf_op | source)
XLA Modules:
  0.0 83.3 jit_solution(4958290255325327891)
XLA Ops:
  0.6 78.8 %exchange.1 = (bf16[3072,1536]{1,0:T(8,128)(2,1)S(1)}, bf16[2,256,768]{2,1,0:T(8,128)(2,1)S(1)}, f32[256,1536]{1,0:T(8,128)S(1)}) custom-call(bf16[256,1536]{1,0:T(8,128)(2,1)} %pre_ref.1, bf16[64,1536]{1,0:T(8,128)(2,1)} %grad_ref.1, bf16[3072,1536]{1,0:T(8,128)(2,1)} %bitcast.2), custom_call_target="tpu_custom_call" | custom-call | tf_op jit(solution)/shard_map/exchange/pallas_call | solution.py:411
  79.5 3.9 %finish.1 = (bf16[256,1536]{1,0:T(8,128)(2,1)}, bf16[3072,1536]{1,0:T(8,128)(2,1)}) custom-call(bf16[3072,1536]{1,0:T(8,128)(2,1)S(1)} %get-tuple-element.7.weight_grad_ref, bf16[2,256,768]{2,1,0:T(8,128)(2,1)S(1)} %get-tuple-element.8.sums_ref, f32[256,1536]{1,0:T(8,128)S(1)} %get-tuple-element.9.slope_ref), custom_call_target="tpu_custom_call" | custom-call | tf_op jit(solution)/shard_map/finish/pallas_call | solution.py:479

commit v2 on v1

--- a/solution.py
+++ b/solution.py
@@ -123,9 +123,6 @@
     to_x = grad_copy(1, gx, gy, {"gx": other_x}, grad_ref)
     to_y = grad_copy(2, gx, gy, {"gy": far_y}, grad_ref)
     to_core = grad_copy(0, gx, gy, {"gy": core}, grad_ref)
-    to_x.start()
-    to_y.start()
-    to_core.start()
 
     def remote(src, dst, send, recv, peer):
         return pltpu.make_async_remote_copy(
@@ -174,10 +171,30 @@
 
     both_ways(0)
     x_hidden(0, gx).start()
+    to_x.start()
+    to_y.start()
+    to_core.start()
     for q in range(groups // 2, groups):
         make_hidden(q)
     both_ways(1)
     x_hidden(1, gx).start()
+
+    far = pick(me, (UP, UP, DOWN, DOWN))
+    near = 1 - far
+
+    def pass_on(way, piece, hop):
+        ag_arrival(way, piece, hop - 1).wait_recv()
+        ag(way, piece, hop).start()
+
+    def pass_first(piece):
+        @pl.when(is_mid)
+        def _():
+            pass_on(far, piece, 1)
+            pass_on(near, piece, 1)
+
+    pass_first(0)
+    x_hidden(0, other_x).wait_recv()
+    both_ways(2)
 
     to_x.wait_recv()
     x_to_y = grad_copy(3, other_x, gy, {"gy": far_y})
@@ -187,25 +204,15 @@
     to_y.wait_recv()
     y_to_core = grad_copy(5, gx, far_y, {"gy": core})
     y_to_core.start()
+    pass_first(1)
+    x_hidden(1, other_x).wait_recv()
+    both_ways(3)
     x_to_y.wait_recv()
     diag_to_core = grad_copy(6, other_x, far_y, {"gy": core})
     diag_to_core.start()
     for copy in (to_core, x_to_core, y_to_core, diag_to_core):
         copy.wait_recv()
     grad_load.wait()
-
-    far = pick(me, (UP, UP, DOWN, DOWN))
-    near = 1 - far
-
-    def pass_on(way, piece, hop):
-        ag_arrival(way, piece, hop - 1).wait_recv()
-        ag(way, piece, hop).start()
-
-    @pl.when(is_mid)
-    def _():
-        for piece in (0, 1):
-            pass_on(far, piece, 1)
-            pass_on(near, piece, 1)
 
     goal = (
         pick(me, (3, 3, 0, 0)),
@@ -273,9 +280,6 @@
     def _():
         rs_first(0, 0)
 
-    for piece in (0, 1):
-        x_hidden(piece, other_x).wait_recv()
-        both_ways(2 + piece)
     lax.fori_loop(tiles, 8 * tiles, compute, 0)
 
     def make_slope(q, carry):
@@ -302,42 +306,42 @@
 
     @pl.when(is_end)
     def _():
-        for piece in (0, 1):
+        for piece in range(4):
             ag(far, piece, 0).wait_send()
         rs_first(0, 1)
         weight_grad(me)
         rs_sent(0, 0)
         rs_first(1, 0)
-        for piece in (2, 3):
-            ag(far, piece, 0).wait_send()
+        rs_sent(0, 1)
         rs_first(1, 1)
         arrived_at_end(0)
         weight_grad(pick(me, (1, 1, 2, 2)))
-        rs_sent(0, 1)
+        rs_sent(1, 0)
         rs_first(2, 0)
-        rs_sent(1, 0)
+        rs_sent(1, 1)
         rs_first(2, 1)
         arrived_at_end(1)
         weight_grad(pick(me, (2, 2, 1, 1)))
 
     @pl.when(is_mid)
     def _():
-        rs_add(0, 0)
-        weight_grad(me)
         for piece in (0, 1):
             pass_on(near, piece, 2)
         for piece in (2, 3):
+            pass_on(far, piece, 1)
+        weight_grad(me)
+        for piece in (2, 3):
             pass_on(near, piece, 1)
-            pass_on(far, piece, 1)
+        rs_add(0, 0)
         weight_grad(pick(me, (0, 0, 3, 3)))
+        for piece in (2, 3):
+            pass_on(near, piece, 2)
         rs_add(0, 1)
         weight_grad(3 - me)
         rs_add(2, 0)
         rs_add(1, 0)
-        for piece in (2, 3):
-            pass_on(near, piece, 2)
+        rs_add(2, 1)
         rs_add(1, 1)
-        rs_add(2, 1)
 
     def settle(piece):
         total = part_piece(3, piece)
@@ -377,7 +381,6 @@
 
     @pl.when(is_end)
     def _():
-        rs_sent(1, 1)
         rs_sent(2, 0)
         rs_sent(2, 1)
 

time: 83.5 us -> 81.4 us (0.975)
  Pallas kernels: 82.7 us -> 79.8 us
    pallas_call x1, Pallas kernels: 78.8 us -> 75.9 us  [exchange(): pl.pallas_call(exchange_kernel, out_shape=(pltpu.VMEM(weight.shape, bf16)...]
where the time goes in v2:
time: 81.4 us; the launch traced here: 80.4 us
  Pallas kernels  79.8 us (98%)
    pallas_call x1, Pallas kernels, exchange(): pl.pallas_call(exchange_kernel, out_shape=(pltpu.VMEM(weight.shape, bf16)...  75.9 us
    pallas_call x1, Pallas kernels, with_kernel(): pl.pallas_call(finish_kernel, out_shape=(pltpu.HBM(pre_act.shape, jnp.bfl...  3.9 us

profile of v2, /device:TPU:17, one launch (start us, length us, event | category | flops | bytes accessed | tf_op | source)
XLA Modules:
  0.0 80.4 jit_solution(2441142172691497477)
XLA Ops:
  0.6 75.9 %exchange.1 = (bf16[3072,1536]{1,0:T(8,128)(2,1)S(1)}, bf16[2,256,768]{2,1,0:T(8,128)(2,1)S(1)}, f32[256,1536]{1,0:T(8,128)S(1)}) custom-call(bf16[256,1536]{1,0:T(8,128)(2,1)} %pre_ref.1, bf16[64,1536]{1,0:T(8,128)(2,1)} %grad_ref.1, bf16[3072,1536]{1,0:T(8,128)(2,1)} %bitcast.2), custom_call_target="tpu_custom_call" | custom-call | tf_op jit(solution)/shard_map/exchange/pallas_call | solution.py:414
  76.5 3.9 %finish.1 = (bf16[256,1536]{1,0:T(8,128)(2,1)}, bf16[3072,1536]{1,0:T(8,128)(2,1)}) custom-call(bf16[3072,1536]{1,0:T(8,128)(2,1)S(1)} %get-tuple-element.7.weight_grad_ref, bf16[2,256,768]{2,1,0:T(8,128)(2,1)S(1)} %get-tuple-element.8.sums_ref, f32[256,1536]{1,0:T(8,128)S(1)} %get-tuple-element.9.slope_ref), custom_call_target="tpu_custom_call" | custom-call | tf_op jit(solution)/shard_map/finish/pallas_call | solution.py:482

commit v3 on v2

--- a/solution.py
+++ b/solution.py
@@ -171,13 +171,13 @@
 
     both_ways(0)
     x_hidden(0, gx).start()
-    to_x.start()
     to_y.start()
     to_core.start()
     for q in range(groups // 2, groups):
         make_hidden(q)
     both_ways(1)
     x_hidden(1, gx).start()
+    to_x.start()
 
     far = pick(me, (UP, UP, DOWN, DOWN))
     near = 1 - far
@@ -196,22 +196,14 @@
     x_hidden(0, other_x).wait_recv()
     both_ways(2)
 
-    to_x.wait_recv()
-    x_to_y = grad_copy(3, other_x, gy, {"gy": far_y})
-    x_to_y.start()
-    x_to_core = grad_copy(4, other_x, gy, {"gy": core})
-    x_to_core.start()
     to_y.wait_recv()
     y_to_core = grad_copy(5, gx, far_y, {"gy": core})
     y_to_core.start()
     pass_first(1)
     x_hidden(1, other_x).wait_recv()
     both_ways(3)
-    x_to_y.wait_recv()
-    diag_to_core = grad_copy(6, other_x, far_y, {"gy": core})
-    diag_to_core.start()
-    for copy in (to_core, x_to_core, y_to_core, diag_to_core):
-        copy.wait_recv()
+    to_core.wait_recv()
+    y_to_core.wait_recv()
     grad_load.wait()
 
     goal = (
@@ -226,7 +218,8 @@
     weight_load.wait()
 
     def compute(index, carry):
-        slot = index // tiles
+        order = index // tiles
+        slot = jnp.where(order < 2, 1 - order, order)
         piece = lax.rem(index, tiles)
         step = slot // 2
         tok = jnp.where(lax.rem(slot, 2) == 0, other_x, gx)
@@ -278,8 +271,24 @@
 
     @pl.when(is_end)
     def _():
-        rs_first(0, 0)
-
+        rs_first(0, 1)
+
+    to_x.wait_recv()
+    x_to_y = grad_copy(3, other_x, gy, {"gy": far_y})
+    x_to_y.start()
+    x_to_core = grad_copy(4, other_x, gy, {"gy": core})
+    x_to_core.start()
+
+    @pl.when(is_mid)
+    def _():
+        for piece in (0, 1):
+            pass_on(near, piece, 2)
+
+    x_to_y.wait_recv()
+    diag_to_core = grad_copy(6, other_x, far_y, {"gy": core})
+    diag_to_core.start()
+    x_to_core.wait_recv()
+    diag_to_core.wait_recv()
     lax.fori_loop(tiles, 8 * tiles, compute, 0)
 
     def make_slope(q, carry):
@@ -308,11 +317,11 @@
     def _():
         for piece in range(4):
             ag(far, piece, 0).wait_send()
-        rs_first(0, 1)
+        rs_first(0, 0)
         weight_grad(me)
+        rs_sent(0, 1)
+        rs_first(1, 0)
         rs_sent(0, 0)
-        rs_first(1, 0)
-        rs_sent(0, 1)
         rs_first(1, 1)
         arrived_at_end(0)
         weight_grad(pick(me, (1, 1, 2, 2)))
@@ -325,18 +334,16 @@
 
     @pl.when(is_mid)
     def _():
-        for piece in (0, 1):
-            pass_on(near, piece, 2)
         for piece in (2, 3):
             pass_on(far, piece, 1)
         weight_grad(me)
         for piece in (2, 3):
             pass_on(near, piece, 1)
-        rs_add(0, 0)
+        rs_add(0, 1)
         weight_grad(pick(me, (0, 0, 3, 3)))
         for piece in (2, 3):
             pass_on(near, piece, 2)
-        rs_add(0, 1)
+        rs_add(0, 0)
         weight_grad(3 - me)
         rs_add(2, 0)
         rs_add(1, 0)
@@ -469,8 +476,10 @@
         )
         total = jnp.dot(pair, select, preferred_element_type=jnp.float32)
         pre_grad[:, span] = (total * slope_ref[:, span]).astype(jnp.bfloat16)
-    copies.append(pltpu.make_async_copy(pre_grad, pre_grad_out, sem.at[4]))
-    copies[-1].start()
+        copies.append(
+            pltpu.make_async_copy(pre_grad.at[:, span], pre_grad_out.at[:, span], sem.at[4 + q])
+        )
+        copies[-1].start()
     for copy in copies:
         copy.wait()
 
@@ -487,7 +496,7 @@
         ),
         in_specs=[anywhere, vmem, vmem],
         out_specs=(anywhere, anywhere),
-        scratch_shapes=[pltpu.VMEM(pre_act.shape, jnp.bfloat16), pltpu.SemaphoreType.DMA((5,))],
+        scratch_shapes=[pltpu.VMEM(pre_act.shape, jnp.bfloat16), pltpu.SemaphoreType.DMA((4 + pre_act.shape[1] // 256,))],
         compiler_params=pltpu.CompilerParams(vmem_limit_bytes=8 * 1024 * 1024),
         name="finish",
     )(weight_grad, sums, slope)

time: 81.4 us -> 88.3 us (1.085)
  Pallas kernels: 79.8 us -> 86.5 us
    pallas_call x1, Pallas kernels: 75.9 us -> 82.5 us  [exchange(): pl.pallas_call(exchange_kernel, out_shape=(pltpu.VMEM(weight.shape, bf16)...]
where the time goes in v3:
time: 88.3 us; the launch traced here: 87.1 us
  Pallas kernels  86.5 us (98%)
    pallas_call x1, Pallas kernels, exchange(): pl.pallas_call(exchange_kernel, out_shape=(pltpu.VMEM(weight.shape, bf16)...  82.5 us
    pallas_call x1, Pallas kernels, with_kernel(): pl.pallas_call(finish_kernel, out_shape=(pltpu.HBM(pre_act.shape, jnp.bfl...  3.92 us

profile of v3, /device:TPU:17, one launch (start us, length us, event | category | flops | bytes accessed | tf_op | source)
XLA Modules:
  0.0 87.1 jit_solution(17639654363216088107)
XLA Ops:
  0.6 82.5 %exchange.1 = (bf16[3072,1536]{1,0:T(8,128)(2,1)S(1)}, bf16[2,256,768]{2,1,0:T(8,128)(2,1)S(1)}, f32[256,1536]{1,0:T(8,128)S(1)}) custom-call(bf16[256,1536]{1,0:T(8,128)(2,1)} %pre_ref.1, bf16[64,1536]{1,0:T(8,128)(2,1)} %grad_ref.1, bf16[3072,1536]{1,0:T(8,128)(2,1)} %bitcast.2), custom_call_target="tpu_custom_call" | custom-call | tf_op jit(solution)/shard_map/exchange/pallas_call | solution.py:421
  83.2 3.9 %finish.1 = (bf16[256,1536]{1,0:T(8,128)(2,1)}, bf16[3072,1536]{1,0:T(8,128)(2,1)}) custom-call(bf16[3072,1536]{1,0:T(8,128)(2,1)S(1)} %get-tuple-element.7.weight_grad_ref, bf16[2,256,768]{2,1,0:T(8,128)(2,1)S(1)} %get-tuple-element.8.sums_ref, f32[256,1536]{1,0:T(8,128)S(1)} %get-tuple-element.9.slope_ref), custom_call_target="tpu_custom_call" | custom-call | tf_op jit(solution)/shard_map/finish/pallas_call | solution.py:491

commit v4 on v3

--- a/solution.py
+++ b/solution.py
@@ -279,17 +279,27 @@
     x_to_core = grad_copy(4, other_x, gy, {"gy": core})
     x_to_core.start()
 
-    @pl.when(is_mid)
-    def _():
-        for piece in (0, 1):
-            pass_on(near, piece, 2)
-
     x_to_y.wait_recv()
     diag_to_core = grad_copy(6, other_x, far_y, {"gy": core})
     diag_to_core.start()
     x_to_core.wait_recv()
     diag_to_core.wait_recv()
-    lax.fori_loop(tiles, 8 * tiles, compute, 0)
+    lax.fori_loop(tiles, 2 * tiles, compute, 0)
+
+    @pl.when(is_end)
+    def _():
+        rs_first(0, 0)
+
+    @pl.when(is_mid)
+    def _():
+        for piece in (0, 1):
+            pass_on(near, piece, 2)
+        for piece in (2, 3):
+            pass_on(far, piece, 1)
+            pass_on(near, piece, 1)
+        rs_add(0, 1)
+
+    lax.fori_loop(2 * tiles, 8 * tiles, compute, 0)
 
     def make_slope(q, carry):
         span = pl.ds(pl.multiple_of(q * group, group), group)
@@ -317,7 +327,6 @@
     def _():
         for piece in range(4):
             ag(far, piece, 0).wait_send()
-        rs_first(0, 0)
         weight_grad(me)
         rs_sent(0, 1)
         rs_first(1, 0)
@@ -334,12 +343,7 @@
 
     @pl.when(is_mid)
     def _():
-        for piece in (2, 3):
-            pass_on(far, piece, 1)
         weight_grad(me)
-        for piece in (2, 3):
-            pass_on(near, piece, 1)
-        rs_add(0, 1)
         weight_grad(pick(me, (0, 0, 3, 3)))
         for piece in (2, 3):
             pass_on(near, piece, 2)

time: 88.3 us -> 78.7 us (0.89)
  Pallas kernels: 86.5 us -> 76.8 us
    pallas_call x1, Pallas kernels: 82.5 us -> 72.8 us  [exchange(): pl.pallas_call(exchange_kernel, out_shape=(pltpu.VMEM(weight.shape, bf16)...]
where the time goes in v4:
time: 78.7 us; the launch traced here: 77.4 us
  Pallas kernels  76.8 us (98%)
    pallas_call x1, Pallas kernels, exchange(): pl.pallas_call(exchange_kernel, out_shape=(pltpu.VMEM(weight.shape, bf16)...  72.8 us
    pallas_call x1, Pallas kernels, with_kernel(): pl.pallas_call(finish_kernel, out_shape=(pltpu.HBM(pre_act.shape, jnp.bfl...  3.92 us

profile of v4, /device:TPU:17, one launch (start us, length us, event | category | flops | bytes accessed | tf_op | source)
XLA Modules:
  0.0 77.4 jit_solution(6044104683788424640)
XLA Ops:
  0.6 72.8 %exchange.1 = (bf16[3072,1536]{1,0:T(8,128)(2,1)S(1)}, bf16[2,256,768]{2,1,0:T(8,128)(2,1)S(1)}, f32[256,1536]{1,0:T(8,128)S(1)}) custom-call(bf16[256,1536]{1,0:T(8,128)(2,1)} %pre_ref.1, bf16[64,1536]{1,0:T(8,128)(2,1)} %grad_ref.1, bf16[3072,1536]{1,0:T(8,128)(2,1)} %bitcast.2), custom_call_target="tpu_custom_call" | custom-call | tf_op jit(solution)/shard_map/exchange/pallas_call | solution.py:425
  73.5 3.9 %finish.1 = (bf16[256,1536]{1,0:T(8,128)(2,1)}, bf16[3072,1536]{1,0:T(8,128)(2,1)}) custom-call(bf16[3072,1536]{1,0:T(8,128)(2,1)S(1)} %get-tuple-element.7.weight_grad_ref, bf16[2,256,768]{2,1,0:T(8,128)(2,1)S(1)} %get-tuple-element.8.sums_ref, f32[256,1536]{1,0:T(8,128)S(1)} %get-tuple-element.9.slope_ref), custom_call_target="tpu_custom_call" | custom-call | tf_op jit(solution)/shard_map/finish/pallas_call | solution.py:495

commit v5 on v4

--- a/solution.py
+++ b/solution.py
@@ -337,9 +337,10 @@
         rs_sent(1, 0)
         rs_first(2, 0)
         rs_sent(1, 1)
-        rs_first(2, 1)
         arrived_at_end(1)
         weight_grad(pick(me, (2, 2, 1, 1)))
+        rs_sent(2, 0)
+        rs_first(2, 1)
 
     @pl.when(is_mid)
     def _():
@@ -351,7 +352,9 @@
         weight_grad(3 - me)
         rs_add(2, 0)
         rs_add(1, 0)
+        rs_sent(2, 0)
         rs_add(2, 1)
+        rs_sent(1, 0)
         rs_add(1, 1)
 
     def settle(piece):
@@ -392,7 +395,6 @@
 
     @pl.when(is_end)
     def _():
-        rs_sent(2, 0)
         rs_sent(2, 1)
 
     @pl.when(is_mid)
@@ -402,8 +404,8 @@
                 ag(far, piece, hop).wait_send()
             for hop in range(3):
                 ag(near, piece, hop).wait_send()
+        rs_sent(0, 0)
         for step in range(3):
-            rs_sent(step, 0)
             rs_sent(step, 1)
 
     for copy in (to_core, to_x, to_y, x_to_y, x_to_core, y_to_core, diag_to_core):

time: 78.7 us -> 78.7 us (level)
  no operation moved by 1% of the time
where the time goes in v5:
time: 78.7 us; the launch traced here: 77.6 us
  Pallas kernels  77 us (98%)
    pallas_call x1, Pallas kernels, exchange(): pl.pallas_call(exchange_kernel, out_shape=(pltpu.VMEM(weight.shape, bf16)...  73.1 us
    pallas_call x1, Pallas kernels, with_kernel(): pl.pallas_call(finish_kernel, out_shape=(pltpu.HBM(pre_act.shape, jnp.bfl...  3.92 us

profile of v5, /device:TPU:17, one launch (start us, length us, event | category | flops | bytes accessed | tf_op | source)
XLA Modules:
  0.0 77.6 jit_solution(12737971367266770381)
XLA Ops:
  0.6 73.1 %exchange.1 = (bf16[3072,1536]{1,0:T(8,128)(2,1)S(1)}, bf16[2,256,768]{2,1,0:T(8,128)(2,1)S(1)}, f32[256,1536]{1,0:T(8,128)S(1)}) custom-call(bf16[256,1536]{1,0:T(8,128)(2,1)} %pre_ref.1, bf16[64,1536]{1,0:T(8,128)(2,1)} %grad_ref.1, bf16[3072,1536]{1,0:T(8,128)(2,1)} %bitcast.2), custom_call_target="tpu_custom_call" | custom-call | tf_op jit(solution)/shard_map/exchange/pallas_call | solution.py:427
  73.7 3.9 %finish.1 = (bf16[256,1536]{1,0:T(8,128)(2,1)}, bf16[3072,1536]{1,0:T(8,128)(2,1)}) custom-call(bf16[3072,1536]{1,0:T(8,128)(2,1)S(1)} %get-tuple-element.7.weight_grad_ref, bf16[2,256,768]{2,1,0:T(8,128)(2,1)S(1)} %get-tuple-element.8.sums_ref, f32[256,1536]{1,0:T(8,128)S(1)} %get-tuple-element.9.slope_ref), custom_call_target="tpu_custom_call" | custom-call | tf_op jit(solution)/shard_map/finish/pallas_call | solution.py:497
